TPU v7x, 32 devices: a whole 2x2x4 slice. The times are simulated.
32 devices in a mesh: row: 2 (over core), lat: 8 (over z, x), grp: 2 (over y).
Axes of the slice: x: 2, y: 2, z: 4, core: 2. Of those that a mesh axis runs over, the one named last changes fastest.
Arguments:
- stream_in: bfloat16 [192, 3584], P(('lat', 'grp'), 'row'), may hold values from -36 to 36, as said below
- pre_gain: float32 [3584], P('row'), may hold values from 0.25 to 1.75
- gate_weight: bfloat16 [3584, 14336], P('row', ('lat', 'grp')), may hold values from -0.09375 to 0.09375
- up_weight: bfloat16 [3584, 14336], P('row', ('lat', 'grp')), may hold values from -0.09375 to 0.09375
- down_weight: bfloat16 [14336, 3584], P(('lat', 'grp'), 'row'), may hold values from -0.046875 to 0.046875
- post_gain: float32 [3584], P('row'), may hold values from 0.25 to 1.75
- enc_weight: float32 [3584, 16384], P('row', ('lat', 'grp')), may hold values from -0.09375 to 0.09375
- enc_bias: float32 [16384], P(('lat', 'grp')), may hold values from -3 to 3
- dec_weight: float32 [16384, 3584], P(('lat', 'grp'), 'row'), may hold values from -0.046875 to 0.046875
- dec_bias: float32 [3584], P('row'), may hold values from -3 to 3
Outputs:
- stream_out: bfloat16 [192, 3584], P(('lat', 'grp'), 'row')
- grad_enc: float32 [3584, 16384], P('row', ('lat', 'grp'))
- grad_enc_bias: float32 [16384], P(('lat', 'grp'))
- grad_dec: float32 [16384, 3584], P(('lat', 'grp'), 'row')
- grad_dec_bias: float32 [3584], P('row')
Inputs may be any that keep to these rules, and one draw needn't show every extreme that they name: `stream_in`: Real-valued activations with scales that differ over rows and features.
All inputs are finite; a program needn't handle non-finite values.
Results may differ from a plain program's by a relative error of at most 0.013.
Values may be sent and summed in bfloat16 or wider, within the bound.
A program may use at most 128 MiB of HBM per device.

v0:
```python
import math
import jax
import jax.numpy as jnp
from jax import lax
from jax.sharding import PartitionSpec as P

D = 3584
epsilon = 1e-06
sparsity = 0.2
sharpness = 4.0


def smooth_relu(value):
    return jax.nn.softplus(sharpness * value) / sharpness


def activate(summed, hidden_width):
    return (
        jax.nn.gelu(summed[:, :hidden_width], approximate=True) * summed[:, hidden_width:]
    ).astype(jnp.bfloat16)


def body(
    stream_in,
    pre_gain,
    gate_weight,
    up_weight,
    down_weight,
    post_gain,
    enc_weight,
    enc_bias,
    dec_weight,
    dec_bias,
):
    highest = lax.Precision.HIGHEST
    stream = stream_in.astype(jnp.float32)
    hidden_width = gate_weight.shape[1]
    squares = lax.psum(jnp.sum(stream * stream, axis=1), "row")
    normed = (stream * lax.rsqrt(squares[:, None] / D + epsilon) * pre_gain).astype(jnp.bfloat16)
    joined = jnp.concatenate([gate_weight, up_weight], axis=1)
    partial_proj = jnp.dot(
        lax.all_gather(normed, ("lat", "grp"), axis=0, tiled=True),
        joined,
        preferred_element_type=jnp.float32,
    )
    shares = lax.psum_scatter(partial_proj, "row", scatter_dimension=0, tiled=True)
    hidden = lax.all_gather(activate(shares, hidden_width), "row", axis=0, tiled=True)
    output = lax.psum_scatter(
        jnp.dot(hidden, down_weight, preferred_element_type=jnp.float32),
        ("lat", "grp"),
        scatter_dimension=0,
        tiled=True,
    )
    out_squares = lax.psum(jnp.sum(output * output, axis=1), "row")
    stream_out = (
        stream + output * lax.rsqrt(out_squares[:, None] / D + epsilon) * post_gain
    ).astype(jnp.bfloat16)
    relayed = lax.all_gather(stream_out, ("lat", "grp"), axis=0, tiled=True)
    inputs = relayed.astype(jnp.float32)
    scale = 1.0 / math.sqrt(inputs.shape[0])
    encoded = jnp.dot(inputs, enc_weight, precision=highest, preferred_element_type=jnp.float32)
    preact = lax.psum(encoded, "row") + enc_bias
    latents = smooth_relu(preact)
    partial_rec = jnp.dot(
        latents, dec_weight, precision=highest, preferred_element_type=jnp.float32
    )
    recon = lax.psum(partial_rec, ("lat", "grp"))
    residual_grad = (recon + dec_bias - inputs) * scale
    grad_dec = jnp.dot(
        latents.T, residual_grad, precision=highest, preferred_element_type=jnp.float32
    )
    grad_dec_bias = jnp.sum(residual_grad, axis=0)
    back_term = jnp.dot(
        residual_grad, dec_weight.T, precision=highest, preferred_element_type=jnp.float32
    )
    latent_grad = (
        lax.psum(back_term.astype(jnp.bfloat16), "row").astype(jnp.float32) + sparsity * scale
    )
    preact_grad = latent_grad * jax.nn.sigmoid(sharpness * preact)
    grad_enc = jnp.dot(inputs.T, preact_grad, precision=highest, preferred_element_type=jnp.float32)
    grad_enc_bias = jnp.sum(preact_grad, axis=0)
    return (stream_out, grad_enc, grad_enc_bias, grad_dec, grad_dec_bias)


def solution(mesh):
    placed = (
        P(("lat", "grp"), "row"),
        P("row"),
        P("row", ("lat", "grp")),
        P("row", ("lat", "grp")),
        P(("lat", "grp"), "row"),
        P("row"),
        P("row", ("lat", "grp")),
        P(("lat", "grp")),
        P(("lat", "grp"), "row"),
        P("row"),
    )
    return jax.shard_map(
        body,
        mesh=mesh,
        in_specs=placed,
        out_specs=(
            P(("lat", "grp"), "row"),
            P("row", ("lat", "grp")),
            P(("lat", "grp")),
            P(("lat", "grp"), "row"),
            P("row"),
        ),
        check_vma=False,
    )
```

profile of v0, /device:TPU:0, one launch (start us, length us, event | category | flops | bytes accessed | tf_op | source)
XLA Modules:
  0.0 402.0 jit_solution(2031803251081122726)
XLA Ops:
  7.2 1.1 fusion.20
  8.3 2.6 psum.35
  10.9 0.9 fusion.24
  11.8 50.0 %all-gather = bf16[16,12,1792]{2,1,0:T(8,128)(2,1)} all-gather(bf16[1,12,1792]{2,1,0:T(8,128)(2,1)S(1)} %fusion.24), channel_id=1, replica_groups=mesh['row'=2,'lat'=8,'grp'=2] {'lat','grp'}, dimensions={0}, use_global_device_ids=true | all-gather | bytes 731136 | tf_op jit(solution)/shard_map/all_gather | solution.py:42
  61.9 2.1 reshape.23
  63.9 5.6 %fusion.1 = f32[192,1792]{1,0:T(8,128)} fusion(bf16[192,1792]{1,0:T(8,128)(2,1)} %reshape.23, bf16[1792,896]{1,0:T(8,128)(2,1)} %param.13, bf16[1792,896]{1,0:T(8,128)(2,1)} %param.12), kind=kOutput, calls=%fused_computation | convolution fusion | flops 1245970432 | bytes 8486912 | tf_op jit(solution)/shard_map/dot_general | solution.py:41
  69.6 4.8 %reduce-scatter.4.cloned.1.call-done = f32[96,1792]{1,0:T(8,128)} async-done(((f32[192,1792]{1,0:T(8,128)}), f32[96,1792]{1,0:T(8,128)}) %reduce-scatter.4.cloned.1.call-update) | async-done | bytes 688144 | tf_op jit(solution)/shard_map/reduce_scatter | solution.py:46
  74.4 1.2 fusion.14
  75.6 2.1 all_gather.10
  77.7 2.0 fusion.36
  79.6 52.9 %fusion = f32[16,1792]{1,0:T(8,128)S(1)} fusion(f32[192,1792]{1,0:T(8,128)} %fusion.36), kind=kCustom, calls=%all-reduce-scatter | all-reduce-scatter fusion | flops 458753 | bytes 1491456
  132.6 1.3 collective-permute-start.2
  133.9 4.5 %collective-permute-start.1 = (f32[16,1792]{1,0:T(8,128)S(1)}, f32[16,1792]{1,0:T(8,128)}, u32[]{:S(2)}, u32[]{:S(2)}) collective-permute-start(f32[16,1792]{1,0:T(8,128)S(1)} %fusion), channel_id=1, source_target_pairs={{0,2},{1,3},{2,4},{3,5},{4,6},{5,7},{6,8},{7,9},{8,10},{9,11},{10,... | collective-permute-start | bytes 344072
  138.4 2.2 collective-permute-start
  141.2 2.4 collective-permute-start.3
  144.8 0.8 collective-permute-done.3
  145.6 8.0 %concatenate.4 = f32[76,1792]{1,0:T(8,128)} concatenate(f32[12,1792]{1,0:T(8,128)} %collective-permute-done.3, f32[16,1792]{1,0:T(8,128)S(1)} %collective-permute-done.2, f32[16,1792]{1,0:T(8,128)} %collective-permute-done.1, f32[16,1792]{1,0:T(8,128)} %collective-permute-done, f32[16,1792]{1,0:T(8,128)S(1)} %fusion), dimensions={0} | concatenate | bytes 1089536
  153.6 1.0 multiply_reduce_fusion
  154.6 2.5 psum.36
  157.1 1.0 fusion.23
  158.2 47.7 %all-gather.1 = bf16[16,12,1792]{2,1,0:T(8,128)(2,1)} all-gather(bf16[1,12,1792]{2,1,0:T(8,128)(2,1)S(1)} %bitcast.14), channel_id=1, replica_groups=mesh['row'=2,'lat'=8,'grp'=2] {'lat','grp'}, dimensions={0}, use_global_device_ids=true | all-gather | bytes 731136 | tf_op jit(solution)/shard_map/all_gather | solution.py:58
  205.8 2.1 reshape.25
  207.9 7.3 %fusion.37 = f32[192,1024]{1,0:T(8,128)} fusion(bf16[192,1792]{1,0:T(8,128)(2,1)} %reshape.25, f32[1792,1024]{1,0:T(8,128)} %param.16), kind=kOutput, calls=%fused_computation.46 | convolution fusion | flops 4227858432 | bytes 8814592 | tf_op jit(solution)/shard_map/dot_general | solution.py:61
  215.5 15.0 %all-reduce.6.cloned.1.call-done = f32[192,1024]{1,0:T(8,128)} async-done(((f32[192,1024]{1,0:T(8,128)}), f32[192,1024]{1,0:T(8,128)}) %all-reduce.6.cloned.1.call-update) | async-done | bytes 786448 | tf_op jit(solution)/shard_map/psum | solution.py:62
  230.5 9.9 %fusion.17 = f32[192,1792]{1,0:T(8,128)} fusion(f32[1024,1792]{1,0:T(8,128)} %param.18, f32[192,1024]{1,0:T(8,128)} %all-reduce.6.cloned.1.call-done, f32[1024]{0:T(1024)S(1)} %copy-done.6), kind=kOutput, calls=%fused_computation.21 | convolution fusion | flops 4229627904 | bytes 9506816 | tf_op jit(solution)/shard_map/dot_general | solution.py:64
  240.7 116.4 %all-reduce.8.cloned.1.call-done = f32[192,1792]{1,0:T(8,128)} async-done(((f32[192,1792]{1,0:T(8,128)}), f32[192,1792]{1,0:T(8,128)}) %all-reduce.8.cloned.1.call-update) | async-done | bytes 1376272 | tf_op jit(solution)/shard_map/psum | solution.py:67
  357.0 12.0 %convolution_convert_fusion = bf16[192,1024]{1,0:T(8,128)(2,1)} fusion(f32[1024,1792]{1,0:T(8,128)} %param.18, bf16[192,1792]{1,0:T(8,128)(2,1)} %reshape.25, f32[192,1792]{1,0:T(8,128)} %all-reduce.8.cloned.1.call-done, f32[1792]{0:T(1024)S(1)} %copy-done.7), kind=kOutput, calls=%fused_computation.6 | convolution fusion | flops 4229431296 | bytes 9804800 | tf_op jit(solution)/shard_map/dot_general | solution.py:73
  369.0 2.5 fusion.19
  371.5 10.1 %fusion.15 = f32[1024,1792]{1,0:T(8,128)} fusion(f32[192,1024]{1,0:T(8,128)S(1)} %copy-done.3, f32[1024]{0:T(1024)S(1)} %copy-done.6, bf16[192,1792]{1,0:T(8,128)(2,1)S(1)} %copy-done.1, f32[192,1792]{1,0:T(8,128)} %all-reduce.8.cloned.1.call-done, f32[1792]{0:T(1024)S(1)} %copy-done.7), kind=kOutput, calls=%fused_computation.20 | convolution fusion | flops 4231004160 | bytes 10202112 | tf_op jit(solution)/shard_map/dot_general | solution.py:69
  381.6 5.0 %all-reduce.10.cloned.1.call-done = bf16[192,1024]{1,0:T(8,128)(2,1)} async-done(((bf16[192,1024]{1,0:T(8,128)(2,1)}), bf16[192,1024]{1,0:T(8,128)(2,1)}) %all-reduce.10.cloned.1.call-update) | async-done | bytes 393232 | tf_op jit(solution)/shard_map/psum | solution.py:77
  386.6 2.2 fusion.34
  388.8 6.7 %fusion.35 = f32[1792,1024]{1,0:T(8,128)} fusion(bf16[192,1792]{1,0:T(8,128)(2,1)S(1)} %copy-done.2, bf16[192,1024]{1,0:T(8,128)(2,1)} %all-reduce.10.cloned.1.call-done, f32[192,1024]{1,0:T(8,128)} %all-reduce.6.cloned.1.call-done, f32[1024]{0:T(1024)S(1)} %copy-done.6), kind=kOutput, calls=%fused_computation.44 | convolution fusion | flops 4229431296 | bytes 9211904 | tf_op jit(solution)/shard_map/dot_general | solution.py:80
  (35 shorter events, 1.9 us)
Async XLA Ops:
  7.2 70.5 %copy-start = (bf16[896,1792]{1,0:T(8,128)(2,1)S(1)}, bf16[896,1792]{1,0:T(8,128)(2,1)}, u32[]{:S(2)}) copy-start(bf16[896,1792]{1,0:T(8,128)(2,1)} %param.14) | copy-start | bytes 9633796
  7.2 67.2 %reduce-scatter.4.cloned.1.call-start = ((), (), s32[]{:S(2)}) async-start(), calls=%async_computation.1 | async-start | bytes 2064384 | tf_op jit(solution)/shard_map/reduce_scatter | solution.py:46
  69.6 160.9 %all-reduce.6.cloned.1.call-start = ((), (), s32[]{:S(2)}) async-start(), calls=%async_computation.2 | async-start | bytes 1572864 | tf_op jit(solution)/shard_map/psum | solution.py:62
  77.7 65.9 %copy-start.9 = (u32[32]{0:T(128)S(1)}, u32[32]{0:T(128)}, u32[]{:S(2)}) copy-start(u32[32]{0:T(128)} %constant.30) | copy-start | bytes 388
  79.6 77.5 %copy-start.4 = (bf16[12,1792]{1,0:T(8,128)(2,1)S(1)}, bf16[12,1792]{1,0:T(8,128)(2,1)}, u32[]{:S(2)}) copy-start(bf16[12,1792]{1,0:T(8,128)(2,1)} %param.10) | copy-start | bytes 129028
  79.6 77.5 %copy-start.8 = (f32[1792]{0:T(1024)S(1)}, f32[1792]{0:T(1024)}, u32[]{:S(2)}) copy-start(f32[1792]{0:T(1024)} %param.15) | copy-start | bytes 21508
  132.6 13.1 %collective-permute-start.2 = (f32[16,1792]{1,0:T(8,128)S(1)}, f32[16,1792]{1,0:T(8,128)S(1)}, u32[]{:S(2)}, u32[]{:S(2)}) collective-permute-start(f32[16,1792]{1,0:T(8,128)S(1)} %fusion), channel_id=1, source_target_pairs={{0,3},{1,4},{2,5},{3,6},{4,7},{5,8},{6,9},{7,10},{8,11},{9,12},{10... | collective-permute-start | bytes 344072
  133.9 11.8 %collective-permute-start.1 = (f32[16,1792]{1,0:T(8,128)S(1)}, f32[16,1792]{1,0:T(8,128)}, u32[]{:S(2)}, u32[]{:S(2)}) collective-permute-start(f32[16,1792]{1,0:T(8,128)S(1)} %fusion), channel_id=1, source_target_pairs={{0,2},{1,3},{2,4},{3,5},{4,6},{5,7},{6,8},{7,9},{8,10},{9,11},{10,... | collective-permute-start | bytes 344072
  138.4 7.3 %collective-permute-start = (f32[16,1792]{1,0:T(8,128)S(1)}, f32[16,1792]{1,0:T(8,128)}, u32[]{:S(2)}, u32[]{:S(2)}) collective-permute-start(f32[16,1792]{1,0:T(8,128)S(1)} %fusion), channel_id=1, source_target_pairs={{0,1},{1,2},{2,3},{3,4},{4,5},{5,6},{6,7},{7,8},{8,9},{9,10},{10,1... | collective-permute-start | bytes 344072
  141.2 4.4 %collective-permute-start.3 = (f32[12,1792]{1,0:T(8,128)}, f32[12,1792]{1,0:T(8,128)}, u32[]{:S(2)}, u32[]{:S(2)}) collective-permute-start(f32[12,1792]{1,0:T(8,128)} %slice.10), channel_id=1, source_target_pairs={{0,4},{1,5},{2,6},{3,7},{4,8},{5,9},{6,10},{7,11},{8,12},{9,13},{1... | collective-permute-start | bytes 258056
  158.1 57.1 %copy-start.5 = (bf16[12,1792]{1,0:T(8,128)(2,1)}, bf16[12,1792]{1,0:T(8,128)(2,1)S(1)}, u32[]{:S(2)}) copy-start(bf16[12,1792]{1,0:T(8,128)(2,1)S(1)} %fusion.23) | copy-start | bytes 129028
  207.9 22.6 %copy-start.6 = (f32[1024]{0:T(1024)S(1)}, f32[1024]{0:T(1024)}, u32[]{:S(2)}) copy-start(f32[1024]{0:T(1024)} %param.17) | copy-start | bytes 12292
  215.3 141.7 %copy-start.7 = (f32[1792]{0:T(1024)S(1)}, f32[1792]{0:T(1024)}, u32[]{:S(2)}) copy-start(f32[1792]{0:T(1024)} %param.19) | copy-start | bytes 21508
  215.3 141.7 %all-reduce.8.cloned.1.call-start = ((), (), s32[]{:S(2)}) async-start(), calls=%async_computation.3 | async-start | bytes 2752512 | tf_op jit(solution)/shard_map/psum | solution.py:67
  240.4 146.2 %all-reduce.10.cloned.1.call-start = ((), (), s32[]{:S(2)}) async-start(), calls=%async_computation.4 | async-start | bytes 786432 | tf_op jit(solution)/shard_map/psum | solution.py:77
  369.0 2.5 copy-start.1
  369.0 2.5 copy-start.3
  386.6 2.2 copy-start.2
Sparse Core Ops, SparseCore 0:
  69.7 4.6 reduce-scatter.3
  215.4 15.0 all-reduce.5
  240.5 116.4 all-reduce.7
  369.1 17.4 all-reduce.9
where the time goes:
time: 403 us; the launch traced here: 402 us
  blocking collectives  158 us (39%)
  waiting for transfers between devices  142 us (35%)
  matrix products  53.5 us (13%)
  between operations  14.5 us (4%)
  local copies, waits for them, and re-layouts  13.4 us (3%)
  starting transfers between devices  10.9 us (3%)
  other arithmetic  9.95 us (2%)
    psum x1, waiting for transfers between devices, body(): recon = lax.psum(partial_rec, ('lat', 'grp'))  116 us
    unnamed x1, blocking collectives  52.9 us
    all_gather x1, blocking collectives, body(): lax.all_gather(normed, ('lat', 'grp'), axis=0, tiled=True)  50 us
    all_gather x1, blocking collectives, body(): relayed = lax.all_gather(stream_out, ('lat', 'grp'), axis=0, tiled=True)  47.7 us
    psum x1, waiting for transfers between devices, body(): preact = lax.psum(encoded, 'row') + enc_bias  15 us
    unnamed x25, local copies, waits for them, and re-layouts  13.4 us
    dot_general x1, matrix products, body(): jnp.dot(residual_grad, dec_weight.T, precision=highest, preferred_element...  12 us
    unnamed x4, starting transfers between devices  10.4 us
  transfers between devices with their start and end apart: 8, of which 5 were waited for; matrix products, arithmetic and copies ran while one was open for 3% of the time, Pallas kernels for 0%

commit v1 on v0

--- a/solution.py
+++ b/solution.py
@@ -55,7 +55,30 @@
     stream_out = (
         stream + output * lax.rsqrt(out_squares[:, None] / D + epsilon) * post_gain
     ).astype(jnp.bfloat16)
-    relayed = lax.all_gather(stream_out, ("lat", "grp"), axis=0, tiled=True)
+    size, index, span = (
+        lax.axis_size(("lat", "grp")),
+        lax.axis_index(("lat", "grp")),
+        stream_out.shape[0],
+    )
+    upward = [(i, (i + 1) % size) for i in range(size)]
+    left = [(i, (i - 1) % size) for i in range(size)]
+    result = jnp.zeros(
+        (*stream_out.shape[:0], size * span, *stream_out.shape[0 + 1 :]), stream_out.dtype
+    )
+    result = lax.dynamic_update_slice_in_dim(result, stream_out, index * span, axis=0)
+    from_left = from_right = stream_out
+    middle = size // 2
+    for step in range(1, middle + 1):
+        from_left = lax.ppermute(from_left, ("lat", "grp"), upward)
+        result = lax.dynamic_update_slice_in_dim(
+            result, from_left, (index - step) % size * span, axis=0
+        )
+        if step < size - middle:
+            from_right = lax.ppermute(from_right, ("lat", "grp"), left)
+            result = lax.dynamic_update_slice_in_dim(
+                result, from_right, (index + step) % size * span, axis=0
+            )
+    relayed = result
     inputs = relayed.astype(jnp.float32)
     scale = 1.0 / math.sqrt(inputs.shape[0])
     encoded = jnp.dot(inputs, enc_weight, precision=highest, preferred_element_type=jnp.float32)

time: 403 us -> 440 us (1.092)
  blocking collectives: 158 us -> 110 us
  starting transfers between devices: 10.9 us -> 48.1 us
  local copies, waits for them, and re-layouts: 13.4 us -> 38.8 us
  waiting for transfers between devices: 142 us -> 164 us
    all_gather x1 -> x0, blocking collectives: 47.7 us -> none  [body(): relayed = lax.all_gather(stream_out, ('lat', 'grp'), axis=0, tiled=True)]
    ppermute x0 -> x15, starting transfers between devices: none -> 37.4 us  [the longest x7 34.6 us: body(): from_right = lax.ppermute(from_right, ('lat', 'grp'), left)]
    dynamic_update_slice x0 -> x16, local copies, waits for them, and re-layouts: none -> 24.8 us  [the longest x8 12.4 us: body(): lax.dynamic_update_slice_in_dim(result, from_left, (index - step) % size...]
    ppermute x0 -> x15, waiting for transfers between devices: none -> 16 us  [the longest x8 15.7 us: body(): from_left = lax.ppermute(from_left, ('lat', 'grp'), upward)]
    psum x1, waiting for transfers between devices: 15 us -> 20.5 us  [body(): preact = lax.psum(encoded, 'row') + enc_bias]
    unnamed x25 -> x36, local copies, waits for them, and re-layouts: 13.4 us -> 13.1 us
  transfers between devices with their start and end apart: 8 -> 23, of which waited for: 5 -> 13; matrix products, arithmetic and copies ran while one was open for 3% -> 9% of each run, Pallas kernels for 0% -> 0%
where the time goes in v1:
time: 440 us; the launch traced here: 439 us
  waiting for transfers between devices  164 us (37%)
  blocking collectives  110 us (25%)
  matrix products  53.5 us (12%)
  starting transfers between devices  48.1 us (11%)
  local copies, waits for them, and re-layouts  38.8 us (9%)
  between operations  14.6 us (3%)
  other arithmetic  9.95 us (2%)
    psum x1, waiting for transfers between devices, body(): recon = lax.psum(partial_rec, ('lat', 'grp'))  117 us
    unnamed x1, blocking collectives  52.9 us
    all_gather x1, blocking collectives, body(): lax.all_gather(normed, ('lat', 'grp'), axis=0, tiled=True)  50 us
    ppermute x7, starting transfers between devices, body(): from_right = lax.ppermute(from_right, ('lat', 'grp'), left)  34.6 us
    psum x1, waiting for transfers between devices, body(): preact = lax.psum(encoded, 'row') + enc_bias  20.5 us
    ppermute x8, waiting for transfers between devices, body(): from_left = lax.ppermute(from_left, ('lat', 'grp'), upward)  15.7 us
    unnamed x36, local copies, waits for them, and re-layouts  13.1 us
    dynamic_update_slice x8, local copies, waits for them, and re-layouts, body(): lax.dynamic_update_slice_in_dim(result, from_left, (index - step) % size...  12.4 us
  transfers between devices with their start and end apart: 23, of which 13 were waited for; matrix products, arithmetic and copies ran while one was open for 9% of the time, Pallas kernels for 0%

profile of v1, /device:TPU:0, one launch (start us, length us, event | category | flops | bytes accessed | tf_op | source)
XLA Modules:
  0.0 438.8 jit_solution(5399708950860993879)
XLA Ops:
  8.3 2.6 psum.35
  11.8 50.0 %all-gather = bf16[16,12,1792]{2,1,0:T(8,128)(2,1)} all-gather(bf16[1,12,1792]{2,1,0:T(8,128)(2,1)S(1)} %fusion.24), channel_id=1, replica_groups=mesh['row'=2,'lat'=8,'grp'=2] {'lat','grp'}, dimensions={0}, use_global_device_ids=true | all-gather | bytes 731136 | tf_op jit(solution)/shard_map/all_gather | solution.py:42
  63.9 5.6 %fusion.1 = f32[192,1792]{1,0:T(8,128)} fusion(bf16[192,1792]{1,0:T(8,128)(2,1)} %reshape.23, bf16[1792,896]{1,0:T(8,128)(2,1)} %param.13, bf16[1792,896]{1,0:T(8,128)(2,1)} %param.12), kind=kOutput, calls=%fused_computation | convolution fusion | flops 1245970432 | bytes 8486912 | tf_op jit(solution)/shard_map/dot_general | solution.py:41
  69.6 4.8 %reduce-scatter.4.cloned.1.call-done = f32[96,1792]{1,0:T(8,128)} async-done(((f32[192,1792]{1,0:T(8,128)}), f32[96,1792]{1,0:T(8,128)}) %reduce-scatter.4.cloned.1.call-update) | async-done | bytes 688144 | tf_op jit(solution)/shard_map/reduce_scatter | solution.py:46
  79.6 52.9 %fusion = f32[16,1792]{1,0:T(8,128)S(1)} fusion(f32[192,1792]{1,0:T(8,128)} %fusion.36), kind=kCustom, calls=%all-reduce-scatter | all-reduce-scatter fusion | flops 458753 | bytes 1491456
  133.9 4.5 %collective-permute-start.16 = (f32[16,1792]{1,0:T(8,128)S(1)}, f32[16,1792]{1,0:T(8,128)}, u32[]{:S(2)}, u32[]{:S(2)}) collective-permute-start(f32[16,1792]{1,0:T(8,128)S(1)} %fusion), channel_id=1, source_target_pairs={{0,2},{1,3},{2,4},{3,5},{4,6},{5,7},{6,8},{7,9},{8,10},{9,11},{10,... | collective-permute-start | bytes 344072
  138.4 2.2 collective-permute-start.15
  141.2 2.4 collective-permute-start.18
  145.6 8.0 %concatenate.4 = f32[76,1792]{1,0:T(8,128)} concatenate(f32[12,1792]{1,0:T(8,128)} %collective-permute-done.18, f32[16,1792]{1,0:T(8,128)S(1)} %collective-permute-done.17, f32[16,1792]{1,0:T(8,128)} %collective-permute-done.16, f32[16,1792]{1,0:T(8,128)} %collective-permute-done.15, f32[16,1792]{1,0:T(8,128)S(1)} %fusion), dimensions={0} | concatenate | bytes 1089536
  154.6 2.5 psum.36
  158.2 2.8 collective-permute-start
  161.0 2.8 collective-permute-start.1
  163.8 2.2 collective-permute-done
  166.4 5.3 %collective-permute-start.3 = (bf16[12,1792]{1,0:T(8,128)(2,1)S(1)}, bf16[12,1792]{1,0:T(8,128)(2,1)S(1)}, u32[]{:S(2)}, u32[]{:S(2)}) collective-permute-start(bf16[12,1792]{1,0:T(8,128)(2,1)S(1)} %collective-permute-done.1), channel_id=1, source_target_pairs={{0,15},{1,0},{2,1},{3,2},{4,3},{5,4},{6,5},{7,6},{8,7},{9,8},{10,9... | collective-permute-start | bytes 129032 | tf_op jit(solution)/shard_map/ppermute | solution.py:77
  173.8 5.6 %collective-permute-start.5 = (bf16[12,1792]{1,0:T(8,128)(2,1)S(1)}, bf16[12,1792]{1,0:T(8,128)(2,1)S(1)}, u32[]{:S(2)}, u32[]{:S(2)}) collective-permute-start(bf16[12,1792]{1,0:T(8,128)(2,1)S(1)} %collective-permute-done.3), channel_id=1, source_target_pairs={{0,15},{1,0},{2,1},{3,2},{4,3},{5,4},{6,5},{7,6},{8,7},{9,8},{10,9... | collective-permute-start | bytes 129032 | tf_op jit(solution)/shard_map/ppermute | solution.py:77
  179.4 2.2 collective-permute-done.4
  181.7 5.6 %collective-permute-start.7 = (bf16[12,1792]{1,0:T(8,128)(2,1)S(1)}, bf16[12,1792]{1,0:T(8,128)(2,1)S(1)}, u32[]{:S(2)}, u32[]{:S(2)}) collective-permute-start(bf16[12,1792]{1,0:T(8,128)(2,1)S(1)} %collective-permute-done.5), channel_id=1, source_target_pairs={{0,15},{1,0},{2,1},{3,2},{4,3},{5,4},{6,5},{7,6},{8,7},{9,8},{10,9... | collective-permute-start | bytes 129032 | tf_op jit(solution)/shard_map/ppermute | solution.py:77
  187.3 2.2 collective-permute-done.6
  190.1 5.1 %collective-permute-start.9 = (bf16[12,1792]{1,0:T(8,128)(2,1)S(1)}, bf16[12,1792]{1,0:T(8,128)(2,1)S(1)}, u32[]{:S(2)}, u32[]{:S(2)}) collective-permute-start(bf16[12,1792]{1,0:T(8,128)(2,1)S(1)} %collective-permute-done.7), channel_id=1, source_target_pairs={{0,15},{1,0},{2,1},{3,2},{4,3},{5,4},{6,5},{7,6},{8,7},{9,8},{10,9... | collective-permute-start | bytes 129032 | tf_op jit(solution)/shard_map/ppermute | solution.py:77
  197.9 5.1 %collective-permute-start.11 = (bf16[12,1792]{1,0:T(8,128)(2,1)S(1)}, bf16[12,1792]{1,0:T(8,128)(2,1)}, u32[]{:S(2)}, u32[]{:S(2)}) collective-permute-start(bf16[12,1792]{1,0:T(8,128)(2,1)S(1)} %collective-permute-done.9), channel_id=1, source_target_pairs={{0,15},{1,0},{2,1},{3,2},{4,3},{5,4},{6,5},{7,6},{8,7},{9,8},{10,9... | collective-permute-start | bytes 129032 | tf_op jit(solution)/shard_map/ppermute | solution.py:77
  203.0 2.6 collective-permute-done.10
  206.2 5.1 %collective-permute-start.13 = (bf16[12,1792]{1,0:T(8,128)(2,1)}, bf16[12,1792]{1,0:T(8,128)(2,1)}, u32[]{:S(2)}, u32[]{:S(2)}) collective-permute-start(bf16[12,1792]{1,0:T(8,128)(2,1)} %collective-permute-done.11), channel_id=1, source_target_pairs={{0,15},{1,0},{2,1},{3,2},{4,3},{5,4},{6,5},{7,6},{8,7},{9,8},{10,9... | collective-permute-start | bytes 129032 | tf_op jit(solution)/shard_map/ppermute | solution.py:77
  239.2 7.3 %fusion.37 = f32[192,1024]{1,0:T(8,128)} fusion(bf16[192,1792]{1,0:T(8,128)(2,1)} %dynamic_update_slice.63, f32[1792,1024]{1,0:T(8,128)} %param.16), kind=kOutput, calls=%fused_computation.46 | convolution fusion | flops 4227858432 | bytes 8814592 | tf_op jit(solution)/shard_map/dot_general | solution.py:84
  246.8 20.5 %all-reduce.6.cloned.1.call-done = f32[192,1024]{1,0:T(8,128)} async-done(((f32[192,1024]{1,0:T(8,128)}), f32[192,1024]{1,0:T(8,128)}) %all-reduce.6.cloned.1.call-update) | async-done | bytes 786448 | tf_op jit(solution)/shard_map/psum | solution.py:85
  267.3 9.9 %fusion.17 = f32[192,1792]{1,0:T(8,128)} fusion(f32[1024,1792]{1,0:T(8,128)} %param.18, f32[192,1024]{1,0:T(8,128)} %all-reduce.6.cloned.1.call-done, f32[1024]{0:T(1024)S(1)} %copy-done.6), kind=kOutput, calls=%fused_computation.21 | convolution fusion | flops 4229627904 | bytes 9506816 | tf_op jit(solution)/shard_map/dot_general | solution.py:87
  277.2 116.6 %all-reduce.8.cloned.1.call-done = f32[192,1792]{1,0:T(8,128)} async-done(((f32[192,1792]{1,0:T(8,128)}), f32[192,1792]{1,0:T(8,128)}) %all-reduce.8.cloned.1.call-update) | async-done | bytes 1376272 | tf_op jit(solution)/shard_map/psum | solution.py:90
  393.8 12.0 %convolution_convert_fusion = bf16[192,1024]{1,0:T(8,128)(2,1)} fusion(f32[1024,1792]{1,0:T(8,128)} %param.18, bf16[192,1792]{1,0:T(8,128)(2,1)} %dynamic_update_slice.63, f32[192,1792]{1,0:T(8,128)} %all-reduce.8.cloned.1.call-done, f32[1792]{0:T(1024)S(1)} %copy-done.7), kind=kOutput, calls=%fused_computation.6 | convolution fusion | flops 4229431296 | bytes 9804800 | tf_op jit(solution)/shard_map/dot_general | solution.py:96
  405.8 2.5 fusion.19
  408.3 10.1 %fusion.15 = f32[1024,1792]{1,0:T(8,128)} fusion(f32[192,1024]{1,0:T(8,128)S(1)} %copy-done.3, f32[1024]{0:T(1024)S(1)} %copy-done.6, bf16[192,1792]{1,0:T(8,128)(2,1)S(1)} %copy-done.1, f32[192,1792]{1,0:T(8,128)} %all-reduce.8.cloned.1.call-done, f32[1792]{0:T(1024)S(1)} %copy-done.7), kind=kOutput, calls=%fused_computation.20 | convolution fusion | flops 4231004160 | bytes 10202112 | tf_op jit(solution)/shard_map/dot_general | solution.py:92
  418.4 5.0 %all-reduce.10.cloned.1.call-done = bf16[192,1024]{1,0:T(8,128)(2,1)} async-done(((bf16[192,1024]{1,0:T(8,128)(2,1)}), bf16[192,1024]{1,0:T(8,128)(2,1)}) %all-reduce.10.cloned.1.call-update) | async-done | bytes 393232 | tf_op jit(solution)/shard_map/psum | solution.py:100
  423.4 2.2 fusion.34
  425.6 6.7 %fusion.35 = f32[1792,1024]{1,0:T(8,128)} fusion(bf16[192,1792]{1,0:T(8,128)(2,1)S(1)} %copy-done.2, bf16[192,1024]{1,0:T(8,128)(2,1)} %all-reduce.10.cloned.1.call-done, f32[192,1024]{1,0:T(8,128)} %all-reduce.6.cloned.1.call-done, f32[1024]{0:T(1024)S(1)} %copy-done.6), kind=kOutput, calls=%fused_computation.44 | convolution fusion | flops 4229431296 | bytes 9211904 | tf_op jit(solution)/shard_map/dot_general | solution.py:103
  (92 shorter events, 49.4 us)
Async XLA Ops:
  7.2 70.5 %copy-start = (bf16[896,1792]{1,0:T(8,128)(2,1)S(1)}, bf16[896,1792]{1,0:T(8,128)(2,1)}, u32[]{:S(2)}) copy-start(bf16[896,1792]{1,0:T(8,128)(2,1)} %param.14) | copy-start | bytes 9633796
  7.2 67.2 %reduce-scatter.4.cloned.1.call-start = ((), (), s32[]{:S(2)}) async-start(), calls=%async_computation.1 | async-start | bytes 2064384 | tf_op jit(solution)/shard_map/reduce_scatter | solution.py:46
  69.6 197.7 %all-reduce.6.cloned.1.call-start = ((), (), s32[]{:S(2)}) async-start(), calls=%async_computation.2 | async-start | bytes 1572864 | tf_op jit(solution)/shard_map/psum | solution.py:85
  77.7 65.9 %copy-start.15 = (u32[32]{0:T(128)S(1)}, u32[32]{0:T(128)}, u32[]{:S(2)}) copy-start(u32[32]{0:T(128)} %constant.145) | copy-start | bytes 388
  79.6 77.5 %copy-start.4 = (bf16[12,1792]{1,0:T(8,128)(2,1)S(1)}, bf16[12,1792]{1,0:T(8,128)(2,1)}, u32[]{:S(2)}) copy-start(bf16[12,1792]{1,0:T(8,128)(2,1)} %param.10) | copy-start | bytes 129028
  79.6 77.5 %copy-start.14 = (f32[1792]{0:T(1024)S(1)}, f32[1792]{0:T(1024)}, u32[]{:S(2)}) copy-start(f32[1792]{0:T(1024)} %param.15) | copy-start | bytes 21508
  132.6 13.1 %collective-permute-start.17 = (f32[16,1792]{1,0:T(8,128)S(1)}, f32[16,1792]{1,0:T(8,128)S(1)}, u32[]{:S(2)}, u32[]{:S(2)}) collective-permute-start(f32[16,1792]{1,0:T(8,128)S(1)} %fusion), channel_id=1, source_target_pairs={{0,3},{1,4},{2,5},{3,6},{4,7},{5,8},{6,9},{7,10},{8,11},{9,12},{10... | collective-permute-start | bytes 344072
  133.9 11.8 %collective-permute-start.16 = (f32[16,1792]{1,0:T(8,128)S(1)}, f32[16,1792]{1,0:T(8,128)}, u32[]{:S(2)}, u32[]{:S(2)}) collective-permute-start(f32[16,1792]{1,0:T(8,128)S(1)} %fusion), channel_id=1, source_target_pairs={{0,2},{1,3},{2,4},{3,5},{4,6},{5,7},{6,8},{7,9},{8,10},{9,11},{10,... | collective-permute-start | bytes 344072
  138.4 7.3 %collective-permute-start.15 = (f32[16,1792]{1,0:T(8,128)S(1)}, f32[16,1792]{1,0:T(8,128)}, u32[]{:S(2)}, u32[]{:S(2)}) collective-permute-start(f32[16,1792]{1,0:T(8,128)S(1)} %fusion), channel_id=1, source_target_pairs={{0,1},{1,2},{2,3},{3,4},{4,5},{5,6},{6,7},{7,8},{8,9},{9,10},{10,1... | collective-permute-start | bytes 344072
  141.2 4.4 %collective-permute-start.18 = (f32[12,1792]{1,0:T(8,128)}, f32[12,1792]{1,0:T(8,128)}, u32[]{:S(2)}, u32[]{:S(2)}) collective-permute-start(f32[12,1792]{1,0:T(8,128)} %slice.10), channel_id=1, source_target_pairs={{0,4},{1,5},{2,6},{3,7},{4,8},{5,9},{6,10},{7,11},{8,12},{9,13},{1... | collective-permute-start | bytes 258056
  158.1 88.4 %copy-start.5 = (bf16[12,1792]{1,0:T(8,128)(2,1)}, bf16[12,1792]{1,0:T(8,128)(2,1)S(1)}, u32[]{:S(2)}) copy-start(bf16[12,1792]{1,0:T(8,128)(2,1)S(1)} %fusion.23) | copy-start | bytes 129028
  158.2 7.9 %collective-permute-start = (bf16[12,1792]{1,0:T(8,128)(2,1)S(1)}, bf16[12,1792]{1,0:T(8,128)(2,1)S(1)}, u32[]{:S(2)}, u32[]{:S(2)}) collective-permute-start(bf16[12,1792]{1,0:T(8,128)(2,1)S(1)} %fusion.23), channel_id=1, source_target_pairs={{0,1},{1,2},{2,3},{3,4},{4,5},{5,6},{6,7},{7,8},{8,9},{9,10},{10,1... | collective-permute-start | bytes 129032 | tf_op jit(solution)/shard_map/ppermute | solution.py:72
  161.0 5.4 %collective-permute-start.1 = (bf16[12,1792]{1,0:T(8,128)(2,1)S(1)}, bf16[12,1792]{1,0:T(8,128)(2,1)S(1)}, u32[]{:S(2)}, u32[]{:S(2)}) collective-permute-start(bf16[12,1792]{1,0:T(8,128)(2,1)S(1)} %fusion.23), channel_id=1, source_target_pairs={{0,15},{1,0},{2,1},{3,2},{4,3},{5,4},{6,5},{7,6},{8,7},{9,8},{10,9... | collective-permute-start | bytes 129032 | tf_op jit(solution)/shard_map/ppermute | solution.py:77
  166.0 7.8 %collective-permute-start.2 = (bf16[12,1792]{1,0:T(8,128)(2,1)S(1)}, bf16[12,1792]{1,0:T(8,128)(2,1)S(1)}, u32[]{:S(2)}, u32[]{:S(2)}) collective-permute-start(bf16[12,1792]{1,0:T(8,128)(2,1)S(1)} %collective-permute-done), channel_id=1, source_target_pairs={{0,1},{1,2},{2,3},{3,4},{4,5},{5,6},{6,7},{7,8},{8,9},{9,10},{10,1... | collective-permute-start | bytes 129032 | tf_op jit(solution)/shard_map/ppermute | solution.py:72
  166.4 7.4 %collective-permute-start.3 = (bf16[12,1792]{1,0:T(8,128)(2,1)S(1)}, bf16[12,1792]{1,0:T(8,128)(2,1)S(1)}, u32[]{:S(2)}, u32[]{:S(2)}) collective-permute-start(bf16[12,1792]{1,0:T(8,128)(2,1)S(1)} %collective-permute-done.1), channel_id=1, source_target_pairs={{0,15},{1,0},{2,1},{3,2},{4,3},{5,4},{6,5},{7,6},{8,7},{9,8},{10,9... | collective-permute-start | bytes 129032 | tf_op jit(solution)/shard_map/ppermute | solution.py:77
  173.8 7.8 %collective-permute-start.4 = (bf16[12,1792]{1,0:T(8,128)(2,1)S(1)}, bf16[12,1792]{1,0:T(8,128)(2,1)S(1)}, u32[]{:S(2)}, u32[]{:S(2)}) collective-permute-start(bf16[12,1792]{1,0:T(8,128)(2,1)S(1)} %collective-permute-done.2), channel_id=1, source_target_pairs={{0,1},{1,2},{2,3},{3,4},{4,5},{5,6},{6,7},{7,8},{8,9},{9,10},{10,1... | collective-permute-start | bytes 129032 | tf_op jit(solution)/shard_map/ppermute | solution.py:72
  173.8 7.8 %collective-permute-start.5 = (bf16[12,1792]{1,0:T(8,128)(2,1)S(1)}, bf16[12,1792]{1,0:T(8,128)(2,1)S(1)}, u32[]{:S(2)}, u32[]{:S(2)}) collective-permute-start(bf16[12,1792]{1,0:T(8,128)(2,1)S(1)} %collective-permute-done.3), channel_id=1, source_target_pairs={{0,15},{1,0},{2,1},{3,2},{4,3},{5,4},{6,5},{7,6},{8,7},{9,8},{10,9... | collective-permute-start | bytes 129032 | tf_op jit(solution)/shard_map/ppermute | solution.py:77
  181.6 7.8 %collective-permute-start.6 = (bf16[12,1792]{1,0:T(8,128)(2,1)S(1)}, bf16[12,1792]{1,0:T(8,128)(2,1)S(1)}, u32[]{:S(2)}, u32[]{:S(2)}) collective-permute-start(bf16[12,1792]{1,0:T(8,128)(2,1)S(1)} %collective-permute-done.4), channel_id=1, source_target_pairs={{0,1},{1,2},{2,3},{3,4},{4,5},{5,6},{6,7},{7,8},{8,9},{9,10},{10,1... | collective-permute-start | bytes 129032 | tf_op jit(solution)/shard_map/ppermute | solution.py:72
  181.7 7.8 %copy-start.8 = (bf16[12,1792]{1,0:T(8,128)(2,1)}, bf16[12,1792]{1,0:T(8,128)(2,1)S(1)}, u32[]{:S(2)}) copy-start(bf16[12,1792]{1,0:T(8,128)(2,1)S(1)} %collective-permute-done.5) | copy-start | bytes 129028
  181.7 7.9 %collective-permute-start.7 = (bf16[12,1792]{1,0:T(8,128)(2,1)S(1)}, bf16[12,1792]{1,0:T(8,128)(2,1)S(1)}, u32[]{:S(2)}, u32[]{:S(2)}) collective-permute-start(bf16[12,1792]{1,0:T(8,128)(2,1)S(1)} %collective-permute-done.5), channel_id=1, source_target_pairs={{0,15},{1,0},{2,1},{3,2},{4,3},{5,4},{6,5},{7,6},{8,7},{9,8},{10,9... | collective-permute-start | bytes 129032 | tf_op jit(solution)/shard_map/ppermute | solution.py:77
  189.5 7.8 %collective-permute-start.8 = (bf16[12,1792]{1,0:T(8,128)(2,1)S(1)}, bf16[12,1792]{1,0:T(8,128)(2,1)S(1)}, u32[]{:S(2)}, u32[]{:S(2)}) collective-permute-start(bf16[12,1792]{1,0:T(8,128)(2,1)S(1)} %collective-permute-done.6), channel_id=1, source_target_pairs={{0,1},{1,2},{2,3},{3,4},{4,5},{5,6},{6,7},{7,8},{8,9},{9,10},{10,1... | collective-permute-start | bytes 129032 | tf_op jit(solution)/shard_map/ppermute | solution.py:72
  190.1 7.2 %collective-permute-start.9 = (bf16[12,1792]{1,0:T(8,128)(2,1)S(1)}, bf16[12,1792]{1,0:T(8,128)(2,1)S(1)}, u32[]{:S(2)}, u32[]{:S(2)}) collective-permute-start(bf16[12,1792]{1,0:T(8,128)(2,1)S(1)} %collective-permute-done.7), channel_id=1, source_target_pairs={{0,15},{1,0},{2,1},{3,2},{4,3},{5,4},{6,5},{7,6},{8,7},{9,8},{10,9... | collective-permute-start | bytes 129032 | tf_op jit(solution)/shard_map/ppermute | solution.py:77
  197.3 8.3 %collective-permute-start.10 = (bf16[12,1792]{1,0:T(8,128)(2,1)S(1)}, bf16[12,1792]{1,0:T(8,128)(2,1)S(1)}, u32[]{:S(2)}, u32[]{:S(2)}) collective-permute-start(bf16[12,1792]{1,0:T(8,128)(2,1)S(1)} %collective-permute-done.8), channel_id=1, source_target_pairs={{0,1},{1,2},{2,3},{3,4},{4,5},{5,6},{6,7},{7,8},{8,9},{9,10},{10,1... | collective-permute-start | bytes 129032 | tf_op jit(solution)/shard_map/ppermute | solution.py:72
  197.9 7.7 %copy-start.12 = (bf16[12,1792]{1,0:T(8,128)(2,1)}, bf16[12,1792]{1,0:T(8,128)(2,1)S(1)}, u32[]{:S(2)}) copy-start(bf16[12,1792]{1,0:T(8,128)(2,1)S(1)} %collective-permute-done.9) | copy-start | bytes 129028
  197.9 7.7 %collective-permute-start.11 = (bf16[12,1792]{1,0:T(8,128)(2,1)S(1)}, bf16[12,1792]{1,0:T(8,128)(2,1)}, u32[]{:S(2)}, u32[]{:S(2)}) collective-permute-start(bf16[12,1792]{1,0:T(8,128)(2,1)S(1)} %collective-permute-done.9), channel_id=1, source_target_pairs={{0,15},{1,0},{2,1},{3,2},{4,3},{5,4},{6,5},{7,6},{8,7},{9,8},{10,9... | collective-permute-start | bytes 129032 | tf_op jit(solution)/shard_map/ppermute | solution.py:77
  205.6 7.9 %collective-permute-start.12 = (bf16[12,1792]{1,0:T(8,128)(2,1)S(1)}, bf16[12,1792]{1,0:T(8,128)(2,1)}, u32[]{:S(2)}, u32[]{:S(2)}) collective-permute-start(bf16[12,1792]{1,0:T(8,128)(2,1)S(1)} %collective-permute-done.10), channel_id=1, source_target_pairs={{0,1},{1,2},{2,3},{3,4},{4,5},{5,6},{6,7},{7,8},{8,9},{9,10},{10,1... | collective-permute-start | bytes 129032 | tf_op jit(solution)/shard_map/ppermute | solution.py:72
  206.2 29.8 %collective-permute-start.13 = (bf16[12,1792]{1,0:T(8,128)(2,1)}, bf16[12,1792]{1,0:T(8,128)(2,1)}, u32[]{:S(2)}, u32[]{:S(2)}) collective-permute-start(bf16[12,1792]{1,0:T(8,128)(2,1)} %collective-permute-done.11), channel_id=1, source_target_pairs={{0,15},{1,0},{2,1},{3,2},{4,3},{5,4},{6,5},{7,6},{8,7},{9,8},{10,9... | collective-permute-start | bytes 129032 | tf_op jit(solution)/shard_map/ppermute | solution.py:77
  213.5 24.1 %collective-permute-start.14 = (bf16[12,1792]{1,0:T(8,128)(2,1)}, bf16[12,1792]{1,0:T(8,128)(2,1)}, u32[]{:S(2)}, u32[]{:S(2)}) collective-permute-start(bf16[12,1792]{1,0:T(8,128)(2,1)} %collective-permute-done.12), channel_id=1, source_target_pairs={{0,1},{1,2},{2,3},{3,4},{4,5},{5,6},{6,7},{7,8},{8,9},{9,10},{10,1... | collective-permute-start | bytes 129032 | tf_op jit(solution)/shard_map/ppermute | solution.py:72
  239.2 28.1 %copy-start.6 = (f32[1024]{0:T(1024)S(1)}, f32[1024]{0:T(1024)}, u32[]{:S(2)}) copy-start(f32[1024]{0:T(1024)} %param.17) | copy-start | bytes 12292
  246.5 147.3 %copy-start.7 = (f32[1792]{0:T(1024)S(1)}, f32[1792]{0:T(1024)}, u32[]{:S(2)}) copy-start(f32[1792]{0:T(1024)} %param.19) | copy-start | bytes 21508
  246.5 147.2 %all-reduce.8.cloned.1.call-start = ((), (), s32[]{:S(2)}) async-start(), calls=%async_computation.3 | async-start | bytes 2752512 | tf_op jit(solution)/shard_map/psum | solution.py:90
  277.2 146.2 %all-reduce.10.cloned.1.call-start = ((), (), s32[]{:S(2)}) async-start(), calls=%async_computation.4 | async-start | bytes 786432 | tf_op jit(solution)/shard_map/psum | solution.py:100
  (7 other events, 16.2 us)
Sparse Core Ops, SparseCore 0:
  69.7 4.6 reduce-scatter.3
  246.7 20.5 all-reduce.5
  277.3 116.4 all-reduce.7
  405.9 17.4 all-reduce.9
